TPU v7x, 512 devices: a whole 4x8x8 slice. The times are simulated.
512 devices in a mesh: ens: 2 (over core), lat: 32 (over z, x), chan: 8 (over y).
Axes of the slice: x: 4, y: 8, z: 8, core: 2. Of those that a mesh axis runs over, the one named last changes fastest.
Arguments:
- field: bfloat16 [2, 384, 128, 256], P('ens', 'chan', 'lat'), may hold values from -6 to 6
- cotangent: bfloat16 [2, 384, 128, 256], P('ens', 'chan', 'lat'), may hold values from -6 to 6
- spec_weight: float32 [2, 64, 384], P(None, None, 'chan'), may hold values from -8 to 8
- disco_coef: float32 [128, 9], replicated, may hold values from -2 to 2
- disco_weight: float32 [9, 384], P(None, 'chan'), may hold values from -5 to 5
- disco_rows: int32 [128, 9], replicated, may hold values from 0 to 127, as said below
- disco_shift: int32 [128, 9], replicated, may hold values from -8 to 8
- w_hidden: bfloat16 [384, 768], replicated, may hold values from -0.3125 to 0.3125
- w_output: bfloat16 [768, 384], replicated, may hold values from -0.21875 to 0.21875
Outputs:
- grad_field: bfloat16 [2, 384, 128, 256], P('ens', 'chan', 'lat')
- grad_spec_weight: float32 [2, 64, 384], P(None, None, 'chan')
- grad_disco_weight: float32 [9, 384], P(None, 'chan')
- grad_w_hidden: float32 [384, 768], P('lat')
- grad_w_output: float32 [768, 384], P('lat')
Inputs may be any that keep to these rules, and one draw needn't show every extreme that they name: Entry k of row i of disco_rows names a latitude row within 2 rows of i.
All inputs are finite; a program needn't handle non-finite values.
Results may differ from a plain program's by a relative error of at most 0.013.
Values may be sent and summed in bfloat16 or wider, within the bound.
A program may use at most 64 MiB of HBM per device.

v0:
```python
import math
import jax
import jax.numpy as jnp
from jax import lax
from jax.sharding import PartitionSpec as P

HALO = 2
SHIFT = 8
norm_eps = 1e-06
inv_root_two = 0.7071067811865476
inv_root_tau = 0.3989422804014327
highest = lax.Precision.HIGHEST


def padded_2(block, sides, width):
    for axis, dim in sides:
        count = lax.axis_size(axis)
        forward = [(i, i + 1) for i in range(count - 1)]
        backward = [(target, source) for source, target in forward]
        low = lax.ppermute(
            lax.slice_in_dim(block, block.shape[dim] - width, None, axis=dim), axis, forward
        )
        high = lax.ppermute(lax.slice_in_dim(block, 0, width, axis=dim), axis, backward)
        block = jnp.concatenate([low, block, high], axis=dim)
    return block


def colatitudes(lat_count):
    return (jnp.arange(lat_count, dtype=jnp.int32).astype(jnp.float32) + 0.5) * (
        math.pi / lat_count
    )


def legendre_rows(first_order, order_count, lat_count, degree_count):
    colatitude = colatitudes(lat_count)
    cosine = jnp.cos(colatitude)
    sine_rows = jnp.sin(colatitude)
    orders = (first_order + jnp.arange(order_count, dtype=jnp.int32)).astype(jnp.float32)
    log_start = 0.5 * (
        jnp.log((2.0 * orders + 1.0) / (4.0 * math.pi))
        + lax.lgamma(orders + 0.5)
        - lax.lgamma(orders + 1.0)
        - 0.5 * math.log(math.pi)
    )
    diagonal = jnp.exp(log_start[:, None] + orders[:, None] * jnp.log(sine_rows)[None, :])

    def advance(carry, degree):
        previous, before = carry
        degree_value = degree.astype(jnp.float32)
        above = degree_value > orders
        upper_term = jnp.where(above, 4.0 * degree_value * degree_value - 1.0, 1.0)
        lower_term = jnp.where(above, degree_value * degree_value - orders * orders, 1.0)
        factor = jnp.sqrt(upper_term / lower_term)
        behind = jnp.where(
            above, (degree_value - 1.0) * (degree_value - 1.0) - orders * orders, 0.0
        )
        damping = jnp.sqrt(behind / (4.0 * (degree_value - 1.0) * (degree_value - 1.0) - 1.0))
        recurred = factor[:, None] * (cosine[None, :] * previous - damping[:, None] * before)
        current = jnp.where(
            above[:, None], recurred, jnp.where((degree_value == orders)[:, None], diagonal, 0.0)
        )
        return ((current, previous), current)

    zero_rows = jnp.zeros((order_count, lat_count), jnp.float32)
    finish, stacked = lax.scan(
        advance, (zero_rows, zero_rows), jnp.arange(degree_count, dtype=jnp.int32), unroll=True
    )
    return jnp.transpose(stacked, (1, 0, 2))


def quadrature(lat_count, lon_count):
    return 2.0 * math.pi / lon_count * (math.pi / lat_count) * jnp.sin(colatitudes(lat_count))


def lon_tables(lon_count, mode_count):
    columns = jnp.arange(lon_count, dtype=jnp.int32)
    mode_ids = jnp.arange(mode_count, dtype=jnp.int32)
    phase_ids = columns[:, None] * mode_ids[None, :] % lon_count
    angles = phase_ids.astype(jnp.float32) * (2.0 * math.pi / lon_count)
    cosine = jnp.cos(angles)
    sine_part = jnp.sin(angles)
    forward = jnp.concatenate([cosine, -sine_part], axis=1).astype(jnp.bfloat16)
    doubled = jnp.where(mode_ids == 0, 1.0, 2.0).astype(jnp.float32)[None, :]
    inverse = jnp.transpose(
        jnp.concatenate([doubled * cosine, -doubled * sine_part], axis=1)
    ).astype(jnp.bfloat16)
    return (forward, inverse)


def apply_filter(coeffs, spec_weight):
    real_weight = jnp.transpose(spec_weight[0])[:, None, :]
    imag_weight = jnp.transpose(spec_weight[1])[:, None, :]
    real_part = coeffs[:, 0]
    imag_part = coeffs[:, 1]
    return jnp.stack(
        [
            real_weight * real_part - imag_weight * imag_part,
            real_weight * imag_part + imag_weight * real_part,
        ],
        axis=1,
    )


def filter_adjoint(grads, coeffs, spec_weight):
    real_weight = jnp.transpose(spec_weight[0])[:, None, :]
    imag_weight = jnp.transpose(spec_weight[1])[:, None, :]
    grad_real = grads[:, 0]
    grad_imag = grads[:, 1]
    real_part = coeffs[:, 0]
    imag_part = coeffs[:, 1]
    weight_zero = jnp.transpose(jnp.sum(grad_real * real_part + grad_imag * imag_part, axis=1))
    weight_one = jnp.transpose(jnp.sum(grad_imag * real_part - grad_real * imag_part, axis=1))
    adjoint_coeffs = jnp.stack(
        [
            real_weight * grad_real + imag_weight * grad_imag,
            real_weight * grad_imag - imag_weight * grad_real,
        ],
        axis=1,
    )
    return (adjoint_coeffs, jnp.stack([weight_zero, weight_one], axis=0))


def mlp_backward(mixed_rows, adjoint_rows, w_hidden, w_output):
    mixed32 = mixed_rows.astype(jnp.float32)
    rscale = lax.rsqrt(jnp.mean(mixed32 * mixed32, axis=0, keepdims=True) + norm_eps)
    normed32 = mixed32 * rscale
    normed = normed32.astype(jnp.bfloat16)
    preact = lax.dot_general(
        w_hidden, normed, (((0,), (0,)), ((), ())), preferred_element_type=jnp.float32
    )
    activated = jax.nn.gelu(preact, approximate=False).astype(jnp.bfloat16)
    grad_output = lax.dot_general(
        activated, adjoint_rows, (((1,), (1,)), ((), ())), preferred_element_type=jnp.float32
    )
    grad_act = lax.dot_general(
        w_output, adjoint_rows, (((1,), (0,)), ((), ())), preferred_element_type=jnp.float32
    )
    cumulative = 0.5 * (1.0 + lax.erf(preact * inv_root_two))
    density = jnp.exp(-0.5 * preact * preact) * inv_root_tau
    grad_pre = (grad_act * (cumulative + preact * density)).astype(jnp.bfloat16)
    grad_hidden = lax.dot_general(
        normed, grad_pre, (((1,), (1,)), ((), ())), preferred_element_type=jnp.float32
    )
    grad_normed = lax.dot_general(
        w_hidden, grad_pre, (((1,), (0,)), ((), ())), preferred_element_type=jnp.float32
    )
    grad_mixed = (
        rscale * (grad_normed - normed32 * jnp.mean(grad_normed * normed32, axis=0, keepdims=True))
    ).astype(jnp.bfloat16)
    return (grad_mixed, grad_hidden, grad_output)


def to_modes(spectrum):
    return lax.all_to_all(spectrum, "lat", split_axis=3, concat_axis=1, tiled=True)


def to_bands(spectrum):
    return lax.all_to_all(spectrum, "lat", split_axis=1, concat_axis=3, tiled=True)


def wrap_lon(values, width):
    return jnp.concatenate([values[:, :, -width:], values, values[:, :, :width]], axis=2)


def disco_kernel(rows_tab, shift_tab, coef_tab, centre, disco_weight):
    row_step = rows_tab - centre[:, None] + HALO
    lon_step = shift_tab + SHIFT
    reach = jnp.arange(2 * HALO + 1, dtype=jnp.int32)
    span = jnp.arange(2 * SHIFT + 1, dtype=jnp.int32)
    onehot = (
        (row_step[:, :, None, None] == reach[None, None, :, None])
        & (lon_step[:, :, None, None] == span[None, None, None, :])
    ).astype(jnp.float32)
    kernel = jnp.einsum("rk,rkpq,kc->crpq", coef_tab, onehot, disco_weight, precision=highest)
    return (onehot, kernel)


def shards(
    field,
    cotangent,
    spec_weight,
    disco_coef,
    disco_weight,
    disco_rows,
    disco_shift,
    w_hidden,
    w_output,
):
    member = field[0]
    adjoint_member = cotangent[0]
    channels, lat_rows, lon_count = member.shape
    band_count = lax.axis_size("lat")
    lat_count = lat_rows * band_count
    mode_count = lat_count // 2
    modes_here = mode_count // band_count
    band_index = lax.axis_index("lat")
    first_row = band_index * lat_rows
    forward, inverse = lon_tables(lon_count, mode_count)
    legendre = legendre_rows(band_index * modes_here, modes_here, lat_count, mode_count)
    weighted = legendre * quadrature(lat_count, lon_count)[None, None, :]
    grad_scale = 1.0 / math.sqrt(lax.axis_size("ens") * lat_count * lon_count)
    reach_count = 2 * HALO + 1
    span_count = 2 * SHIFT + 1
    adjoint_rows = lax.all_to_all(adjoint_member, "chan", split_axis=2, concat_axis=0, tiled=True)
    spectrum = jnp.dot(
        member.reshape(channels * lat_rows, lon_count), forward, preferred_element_type=jnp.float32
    )
    spectrum = spectrum.astype(jnp.bfloat16).reshape(channels, lat_rows, 2, mode_count)
    mode_block = to_modes(spectrum)
    coeffs = jnp.einsum(
        "citm,mli->ctml", mode_block.astype(jnp.float32), weighted, precision=highest
    )
    synthesis = jnp.einsum(
        "ctml,mli->citm", apply_filter(coeffs, spec_weight), legendre, precision=highest
    ).astype(jnp.bfloat16)
    band_block = to_bands(synthesis)
    spectral = jnp.dot(
        band_block.reshape(channels * lat_rows, 2 * mode_count),
        inverse,
        preferred_element_type=jnp.float32,
    )
    spectral = spectral.reshape(channels, lat_rows, lon_count)
    global_rows = first_row + jnp.arange(lat_rows, dtype=jnp.int32)
    rows_here = lax.dynamic_slice_in_dim(disco_rows, first_row, lat_rows, 0)
    shift_here = lax.dynamic_slice_in_dim(disco_shift, first_row, lat_rows, 0)
    coef_here = lax.dynamic_slice_in_dim(disco_coef, first_row, lat_rows, 0)
    onehot_here, kernel_here = disco_kernel(
        rows_here, shift_here, coef_here, global_rows, disco_weight
    )
    padded = padded_2(member, (("lat", 1),), HALO)
    wide_field = wrap_lon(padded, SHIFT)
    disco_out = jnp.zeros((channels, lat_rows, lon_count), jnp.float32)
    for reach in range(reach_count):
        for span in range(span_count):
            window = wide_field[:, reach : reach + lat_rows, span : span + lon_count].astype(
                jnp.float32
            )
            disco_out = disco_out + kernel_here[:, :, reach, span][:, :, None] * window
    mixed_field = (spectral + disco_out).astype(jnp.bfloat16)
    mixed_rows = lax.all_to_all(mixed_field, "chan", split_axis=2, concat_axis=0, tiled=True)
    all_channels = mixed_rows.shape[0]
    row_width = mixed_rows.shape[2]
    grad_rows, grad_hidden, grad_output = mlp_backward(
        mixed_rows.reshape(all_channels, lat_rows * row_width),
        adjoint_rows.reshape(all_channels, lat_rows * row_width),
        w_hidden,
        w_output,
    )
    grad_field = lax.all_to_all(
        grad_rows.reshape(all_channels, lat_rows, row_width),
        "chan",
        split_axis=0,
        concat_axis=2,
        tiled=True,
    )
    grad_synth = lax.dot_general(
        grad_field.reshape(channels * lat_rows, lon_count),
        inverse,
        (((1,), (1,)), ((), ())),
        preferred_element_type=jnp.float32,
    )
    grad_synth = grad_synth.astype(jnp.bfloat16).reshape(channels, lat_rows, 2, mode_count)
    grad_modes = to_modes(grad_synth)
    grad_filtered = jnp.einsum(
        "citm,mli->ctml", grad_modes.astype(jnp.float32), legendre, precision=highest
    )
    grad_coeffs, filter_part = filter_adjoint(grad_filtered, coeffs, spec_weight)
    grad_spectrum = jnp.einsum("ctml,mli->citm", grad_coeffs, weighted, precision=highest).astype(
        jnp.bfloat16
    )
    grad_lines = to_bands(grad_spectrum)
    spectral_back = lax.dot_general(
        grad_lines.reshape(channels * lat_rows, 2 * mode_count),
        forward,
        (((1,), (1,)), ((), ())),
        preferred_element_type=jnp.float32,
    )
    spectral_back = spectral_back.reshape(channels, lat_rows, lon_count)
    grad_wide = grad_field.astype(jnp.float32)
    reach_sums = []
    for reach in range(reach_count):
        span_sums = []
        for span in range(span_count):
            window = wide_field[:, reach : reach + lat_rows, span : span + lon_count].astype(
                jnp.float32
            )
            span_sums.append(jnp.sum(window * grad_wide, axis=2))
        reach_sums.append(jnp.stack(span_sums, axis=2))
    inner_sum = jnp.stack(reach_sums, axis=2)
    disco_part = jnp.einsum(
        "ik,ikpq,cipq->kc", coef_here, onehot_here, inner_sum, precision=highest
    )
    rimmed = padded_2(grad_field, (("lat", 1),), HALO)
    wide_grads = wrap_lon(rimmed, SHIFT)
    ext_count = lat_rows + 2 * HALO
    ext_rows = first_row - HALO + jnp.arange(ext_count, dtype=jnp.int32)
    rows_ext = lax.dynamic_slice_in_dim(
        jnp.pad(disco_rows, ((HALO, HALO), (0, 0))), first_row, ext_count, 0
    )
    shift_ext = lax.dynamic_slice_in_dim(
        jnp.pad(disco_shift, ((HALO, HALO), (0, 0))), first_row, ext_count, 0
    )
    coef_ext = lax.dynamic_slice_in_dim(
        jnp.pad(disco_coef, ((HALO, HALO), (0, 0))), first_row, ext_count, 0
    )
    onehot_ext, kernel_ext = disco_kernel(rows_ext, shift_ext, coef_ext, ext_rows, disco_weight)
    spread = jnp.zeros((channels, lat_rows, lon_count), jnp.float32)
    for reach in range(reach_count):
        row_start = 2 * HALO - reach
        for span in range(span_count):
            col_start = 2 * SHIFT - span
            window = wide_grads[
                :, row_start : row_start + lat_rows, col_start : col_start + lon_count
            ].astype(jnp.float32)
            spread = (
                spread
                + kernel_ext[:, row_start : row_start + lat_rows, reach, span][:, :, None] * window
            )
    grad_input = (adjoint_member.astype(jnp.float32) + spectral_back + spread).astype(jnp.bfloat16)
    filter_total, disco_total = lax.psum((filter_part, disco_part), ("ens", "lat"))
    total_hidden, total_output = lax.psum((grad_hidden, grad_output), ("ens", "lat", "chan"))
    hidden_rows = total_hidden.shape[0] // band_count
    output_rows = total_output.shape[0] // band_count
    share_hidden = lax.dynamic_slice_in_dim(total_hidden, band_index * hidden_rows, hidden_rows, 0)
    share_output = lax.dynamic_slice_in_dim(total_output, band_index * output_rows, output_rows, 0)
    return (
        grad_input[None],
        filter_total,
        disco_total * grad_scale,
        share_hidden * grad_scale,
        share_output * grad_scale,
    )


def solution(mesh):
    in_specs = (
        P("ens", "chan", "lat", None),
        P("ens", "chan", "lat", None),
        P(None, None, "chan"),
        P(),
        P(None, "chan"),
        P(),
        P(),
        P(),
        P(),
    )
    out_specs = (
        P("ens", "chan", "lat", None),
        P(None, None, "chan"),
        P(None, "chan"),
        P("lat", None),
        P("lat", None),
    )
    return jax.shard_map(shards, mesh=mesh, in_specs=in_specs, out_specs=out_specs, check_vma=False)
```

profile of v0, /device:TPU:256, one launch (start us, length us, event | category | flops | bytes accessed | tf_op | source)
XLA Modules:
  0.0 485.7 jit_solution(5748793667730272015)
XLA Ops:
  9.7 9.9 %all-to-all-start = ((bf16[32,2,384]{2,1,0:T(2,128)(2,1)}), bf16[32,2,384]{2,1,0:T(2,128)(2,1)S(1)}, u32[]{:S(2)}, u32[]{:S(2)}) async-start(bf16[32,2,384]{2,1,0:T(2,128)(2,1)} %reshape.55196), calls=%async_computation | async-start | bytes 98304 | tf_op jit(solution)/shard_map/all_to_all | solution.py:154
  19.6 3.4 collective-permute-start
  23.0 5.8 %collective-permute-start.1 = (bf16[48,2,256]{2,0,1:T(8,128)(2,1)S(1)}, bf16[48,2,256]{2,0,1:T(8,128)(2,1)S(1)}, u32[]{:S(2)}, u32[]{:S(2)}) collective-permute-start(bf16[48,2,256]{2,0,1:T(8,128)(2,1)S(1)} %get-tuple-element.536), channel_id=1, source_target_pairs={{8,0},{16,8},{24,16},{32,24},{40,32},{48,40},{56,48},{64,56},{72,6... | collective-permute-start | bytes 147464 | tf_op jit(solution)/shard_map/ppermute | solution.py:23
  89.2 7.4 %all-to-all-start.1 = ((bf16[32,2,384]{2,1,0:T(2,128)(2,1)}), bf16[32,2,384]{2,1,0:T(2,128)(2,1)S(1)}, u32[]{:S(2)}, u32[]{:S(2)}) async-start(bf16[32,2,384]{2,1,0:T(2,128)(2,1)} %reshape.55198), calls=%async_computation.1 | async-start | bytes 98304 | tf_op jit(solution)/shard_map/all_to_all | solution.py:158
  96.8 4.9 %all-to-all-done.1 = bf16[32,2,384]{2,1,0:T(2,128)(2,1)S(1)} async-done(((bf16[32,2,384]{2,1,0:T(2,128)(2,1)}), bf16[32,2,384]{2,1,0:T(2,128)(2,1)S(1)}, u32[]{:S(2)}, u32[]{:S(2)}) %all-to-all-start.1) | async-done | bytes 49184 | tf_op jit(solution)/shard_map/all_to_all | solution.py:158
  101.7 7.1 %all-to-all-start.3 = ((bf16[8,2,3072]{2,1,0:T(2,128)(2,1)}), bf16[8,2,3072]{2,1,0:T(2,128)(2,1)S(1)}, u32[]{:S(2)}, u32[]{:S(2)}) async-start(bf16[8,2,3072]{2,1,0:T(2,128)(2,1)} %reshape.55202), calls=%async_computation.3 | async-start | bytes 196608 | tf_op jit(solution)/shard_map/all_to_all | solution.py:204
  109.5 6.0 %fusion.2 = bf16[48,4,256]{2,0,1:T(8,128)(2,1)S(1)} fusion(bf16[48,4,128]{0,2,1:T(8,128)(2,1)S(1)} %bitcast.623, bf16[48,4,256]{2,0,1:T(8,128)(2,1)S(1)} %bitcast.596, f32[48,4]{0,1:T(4,128)S(1)} %bitcast.820, f32[48,4]{0,1:T(4,128)S(1)} %bitcast.821, f32[48,4]{0,1:T(4,128)S(1)} %bitcast.822, f32[48,4]{0,1:T(4,128)S(1)} %bitcast.823, ...), kind=kOutput, calls=%fused_computation.173 | convolution fusion | flops 25493504 | bytes 8339200 | tf_op jit(solution)/shard_map/dot_general | solution.py:217
  117.6 6.4 %all-to-all-start.2 = ((bf16[8,2,3072]{2,1,0:T(2,128)(2,1)}), bf16[8,2,3072]{2,1,0:T(2,128)(2,1)S(1)}, u32[]{:S(2)}, u32[]{:S(2)}) async-start(bf16[8,2,3072]{2,1,0:T(2,128)(2,1)} %reshape.55200), calls=%async_computation.2 | async-start | bytes 196608 | tf_op jit(solution)/shard_map/all_to_all | solution.py:240
  125.2 7.5 %all-to-all-done.2 = bf16[8,2,3072]{2,1,0:T(2,128)(2,1)S(1)} async-done(((bf16[8,2,3072]{2,1,0:T(2,128)(2,1)}), bf16[8,2,3072]{2,1,0:T(2,128)(2,1)S(1)}, u32[]{:S(2)}, u32[]{:S(2)}) %all-to-all-start.2) | async-done | bytes 98336 | tf_op jit(solution)/shard_map/all_to_all | solution.py:240
  134.6 2.0 fusion.24
  138.8 3.4 all-to-all-start.4
  142.5 1.5 fusion.613
  144.0 6.9 %all-to-all-done.4 = bf16[8,2,3072]{2,1,0:T(2,128)(2,1)S(1)} async-done(((bf16[8,2,3072]{2,1,0:T(2,128)(2,1)}), bf16[8,2,3072]{2,1,0:T(2,128)(2,1)S(1)}, u32[]{:S(2)}, u32[]{:S(2)}) %all-to-all-start.4) | async-done | bytes 98336 | tf_op jit(solution)/shard_map/all_to_all | solution.py:249
  152.1 1.1 fusion.210
  153.2 1.2 fusion.219
  155.5 1.2 fusion.218
  158.3 8.6 %all-to-all-start.5 = ((bf16[32,2,384]{2,1,0:T(2,128)(2,1)}), bf16[32,2,384]{2,1,0:T(2,128)(2,1)S(1)}, u32[]{:S(2)}, u32[]{:S(2)}) async-start(bf16[32,2,384]{2,1,0:T(2,128)(2,1)} %reshape.55206), calls=%async_computation.5 | async-start | bytes 98304 | tf_op jit(solution)/shard_map/all_to_all | solution.py:154
  166.9 3.4 collective-permute-start.2
  170.3 5.8 %collective-permute-start.3 = (bf16[48,2,256]{2,0,1:T(8,128)(2,1)S(1)}, bf16[48,2,256]{2,0,1:T(8,128)(2,1)S(1)}, u32[]{:S(2)}, u32[]{:S(2)}) collective-permute-start(bf16[48,2,256]{2,0,1:T(8,128)(2,1)S(1)} %get-tuple-element.534), channel_id=1, source_target_pairs={{8,0},{16,8},{24,16},{32,24},{40,32},{48,40},{56,48},{64,56},{72,6... | collective-permute-start | bytes 147464 | tf_op jit(solution)/shard_map/ppermute | solution.py:23
  180.3 10.2 %all-to-all-start.6 = ((bf16[32,2,384]{2,1,0:T(2,128)(2,1)}), bf16[32,2,384]{2,1,0:T(2,128)(2,1)S(1)}, u32[]{:S(2)}, u32[]{:S(2)}) async-start(bf16[32,2,384]{2,1,0:T(2,128)(2,1)} %reshape.55208), calls=%async_computation.6 | async-start | bytes 98304 | tf_op jit(solution)/shard_map/all_to_all | solution.py:158
  190.5 276.9 %all-reduce.4 = (f32[2,64,48]{1,2,0:T(8,128)}, f32[9,48]{1,0:T(8,128)S(1)}) all-reduce(f32[2,64,48]{1,2,0:T(8,128)S(1)} %pad_maximum_fusion.8, f32[9,48]{1,0:T(8,128)S(1)} %convolution_bitcast_fusion.6), channel_id=1, replica_groups=mesh['ens'=2,'lat'=32,'chan'=8] {'ens','lat'}, use_global_device_ids=true, to_apply=%region_5.6 | all-reduce | flops 6576 | bytes 52608 | tf_op jit(solution)/shard_map/psum | solution.py:320
  468.7 6.5 %fusion.4 = bf16[1,48,4,256]{3,1,2,0:T(8,128)(2,1)S(1)} fusion(bf16[48,4,128]{0,2,1:T(8,128)(2,1)S(1)} %bitcast.622, bf16[48,4,256]{2,0,1:T(8,128)(2,1)S(1)} %all_to_all.100, bf16[48,8,256]{2,0,1:T(8,128)(2,1)S(1)} %get-tuple-element.539, bf16[48,8,8]{2,0,1:T(8,128)(2,1)S(1)} %get-tuple-element.520, bf16[48,8,8]{2,0,1:T(8,128)(2,1)S(1)} %get-tuple-element.519, ...), kind=kOutput, calls=%fused_computation.177 | convolution fusion | flops 37191680 | bytes 1076992 | tf_op jit(solution)/shard_map/dot_general | solution.py:272
  475.9 1.5 dynamic-slice_multiply_fusion
  477.5 1.4 dynamic-slice_multiply_fusion.1
  (449 shorter events, 37.7 us)
Async XLA Ops:
  9.7 77.4 %all-to-all-start = ((bf16[32,2,384]{2,1,0:T(2,128)(2,1)}), bf16[32,2,384]{2,1,0:T(2,128)(2,1)S(1)}, u32[]{:S(2)}, u32[]{:S(2)}) async-start(bf16[32,2,384]{2,1,0:T(2,128)(2,1)} %reshape.55196), calls=%async_computation | async-start | bytes 98304 | tf_op jit(solution)/shard_map/all_to_all | solution.py:154
  19.6 67.3 %collective-permute-start = (bf16[48,2,256]{2,0,1:T(8,128)(2,1)S(1)}, bf16[48,2,256]{2,0,1:T(8,128)(2,1)S(1)}, u32[]{:S(2)}, u32[]{:S(2)}) collective-permute-start(bf16[48,2,256]{2,0,1:T(8,128)(2,1)S(1)} %get-tuple-element.537), channel_id=1, source_target_pairs={{0,8},{8,16},{16,24},{24,32},{32,40},{40,48},{48,56},{56,64},{64,7... | collective-permute-start | bytes 147464 | tf_op jit(solution)/shard_map/ppermute | solution.py:20
  23.0 63.9 %collective-permute-start.1 = (bf16[48,2,256]{2,0,1:T(8,128)(2,1)S(1)}, bf16[48,2,256]{2,0,1:T(8,128)(2,1)S(1)}, u32[]{:S(2)}, u32[]{:S(2)}) collective-permute-start(bf16[48,2,256]{2,0,1:T(8,128)(2,1)S(1)} %get-tuple-element.536), channel_id=1, source_target_pairs={{8,0},{16,8},{24,16},{32,24},{40,32},{48,40},{56,48},{64,56},{72,6... | collective-permute-start | bytes 147464 | tf_op jit(solution)/shard_map/ppermute | solution.py:23
  89.2 12.5 %all-to-all-start.1 = ((bf16[32,2,384]{2,1,0:T(2,128)(2,1)}), bf16[32,2,384]{2,1,0:T(2,128)(2,1)S(1)}, u32[]{:S(2)}, u32[]{:S(2)}) async-start(bf16[32,2,384]{2,1,0:T(2,128)(2,1)} %reshape.55198), calls=%async_computation.1 | async-start | bytes 98304 | tf_op jit(solution)/shard_map/all_to_all | solution.py:158
  101.7 15.8 %all-to-all-start.3 = ((bf16[8,2,3072]{2,1,0:T(2,128)(2,1)}), bf16[8,2,3072]{2,1,0:T(2,128)(2,1)S(1)}, u32[]{:S(2)}, u32[]{:S(2)}) async-start(bf16[8,2,3072]{2,1,0:T(2,128)(2,1)} %reshape.55202), calls=%async_computation.3 | async-start | bytes 196608 | tf_op jit(solution)/shard_map/all_to_all | solution.py:204
  117.6 15.1 %all-to-all-start.2 = ((bf16[8,2,3072]{2,1,0:T(2,128)(2,1)}), bf16[8,2,3072]{2,1,0:T(2,128)(2,1)S(1)}, u32[]{:S(2)}, u32[]{:S(2)}) async-start(bf16[8,2,3072]{2,1,0:T(2,128)(2,1)} %reshape.55200), calls=%async_computation.2 | async-start | bytes 196608 | tf_op jit(solution)/shard_map/all_to_all | solution.py:240
  138.8 12.0 %all-to-all-start.4 = ((bf16[8,2,3072]{2,1,0:T(2,128)(2,1)}), bf16[8,2,3072]{2,1,0:T(2,128)(2,1)S(1)}, u32[]{:S(2)}, u32[]{:S(2)}) async-start(bf16[8,2,3072]{2,1,0:T(2,128)(2,1)} %reshape.55204), calls=%async_computation.4 | async-start | bytes 196608 | tf_op jit(solution)/shard_map/all_to_all | solution.py:249
  142.2 333.7 %all-reduce.7.cloned.1.call-start = ((), (), s32[]{:S(2)}) async-start(), calls=%async_computation.7 | async-start | bytes 4718592 | tf_op jit(solution)/shard_map/psum | solution.py:321
  158.3 19.9 %all-to-all-start.5 = ((bf16[32,2,384]{2,1,0:T(2,128)(2,1)}), bf16[32,2,384]{2,1,0:T(2,128)(2,1)S(1)}, u32[]{:S(2)}, u32[]{:S(2)}) async-start(bf16[32,2,384]{2,1,0:T(2,128)(2,1)} %reshape.55206), calls=%async_computation.5 | async-start | bytes 98304 | tf_op jit(solution)/shard_map/all_to_all | solution.py:154
  166.9 11.1 %collective-permute-start.2 = (bf16[48,2,256]{2,0,1:T(8,128)(2,1)S(1)}, bf16[48,2,256]{2,0,1:T(8,128)(2,1)S(1)}, u32[]{:S(2)}, u32[]{:S(2)}) collective-permute-start(bf16[48,2,256]{2,0,1:T(8,128)(2,1)S(1)} %get-tuple-element.535), channel_id=1, source_target_pairs={{0,8},{8,16},{16,24},{24,32},{32,40},{40,48},{48,56},{56,64},{64,7... | collective-permute-start | bytes 147464 | tf_op jit(solution)/shard_map/ppermute | solution.py:20
  170.3 7.8 %collective-permute-start.3 = (bf16[48,2,256]{2,0,1:T(8,128)(2,1)S(1)}, bf16[48,2,256]{2,0,1:T(8,128)(2,1)S(1)}, u32[]{:S(2)}, u32[]{:S(2)}) collective-permute-start(bf16[48,2,256]{2,0,1:T(8,128)(2,1)S(1)} %get-tuple-element.534), channel_id=1, source_target_pairs={{8,0},{16,8},{24,16},{32,24},{40,32},{48,40},{56,48},{64,56},{72,6... | collective-permute-start | bytes 147464 | tf_op jit(solution)/shard_map/ppermute | solution.py:23
  178.8 289.6 %copy-start.7 = (f32[48,4,1,1]{0,3,2,1:T(1,128)S(1)}, f32[48,4,1,1]{0,3,2,1:T(1,128)}, u32[]{:S(2)}) copy-start(f32[48,4,1,1]{0,3,2,1:T(1,128)} %get-tuple-element.400) | copy-start | bytes 2308
  178.8 289.6 %copy-start.8 = (f32[48,4,1,1]{0,3,2,1:T(1,128)S(1)}, f32[48,4,1,1]{0,3,2,1:T(1,128)}, u32[]{:S(2)}) copy-start(f32[48,4,1,1]{0,3,2,1:T(1,128)} %get-tuple-element.401) | copy-start | bytes 2308
  178.8 289.6 %copy-start.9 = (f32[48,4,1,1]{0,3,2,1:T(1,128)S(1)}, f32[48,4,1,1]{0,3,2,1:T(1,128)}, u32[]{:S(2)}) copy-start(f32[48,4,1,1]{0,3,2,1:T(1,128)} %get-tuple-element.402) | copy-start | bytes 2308
  178.8 289.6 %copy-start.10 = (f32[48,4,1,1]{0,3,2,1:T(1,128)S(1)}, f32[48,4,1,1]{0,3,2,1:T(1,128)}, u32[]{:S(2)}) copy-start(f32[48,4,1,1]{0,3,2,1:T(1,128)} %get-tuple-element.403) | copy-start | bytes 2308
  178.8 289.6 %copy-start.11 = (f32[48,4,1,1]{0,3,2,1:T(1,128)S(1)}, f32[48,4,1,1]{0,3,2,1:T(1,128)}, u32[]{:S(2)}) copy-start(f32[48,4,1,1]{0,3,2,1:T(1,128)} %get-tuple-element.404) | copy-start | bytes 2308
  178.8 289.6 %copy-start.12 = (f32[48,4,1,1]{0,3,2,1:T(1,128)S(1)}, f32[48,4,1,1]{0,3,2,1:T(1,128)}, u32[]{:S(2)}) copy-start(f32[48,4,1,1]{0,3,2,1:T(1,128)} %get-tuple-element.405) | copy-start | bytes 2308
  178.8 289.6 %copy-start.13 = (f32[48,4,1,1]{0,3,2,1:T(1,128)S(1)}, f32[48,4,1,1]{0,3,2,1:T(1,128)}, u32[]{:S(2)}) copy-start(f32[48,4,1,1]{0,3,2,1:T(1,128)} %get-tuple-element.406) | copy-start | bytes 2308
  178.8 289.6 %copy-start.14 = (f32[48,4,1,1]{0,3,2,1:T(1,128)S(1)}, f32[48,4,1,1]{0,3,2,1:T(1,128)}, u32[]{:S(2)}) copy-start(f32[48,4,1,1]{0,3,2,1:T(1,128)} %get-tuple-element.407) | copy-start | bytes 2308
  178.9 289.6 %copy-start.15 = (f32[48,4,1,1]{0,3,2,1:T(1,128)S(1)}, f32[48,4,1,1]{0,3,2,1:T(1,128)}, u32[]{:S(2)}) copy-start(f32[48,4,1,1]{0,3,2,1:T(1,128)} %get-tuple-element.408) | copy-start | bytes 2308
  178.9 289.6 %copy-start.16 = (f32[48,4,1,1]{0,3,2,1:T(1,128)S(1)}, f32[48,4,1,1]{0,3,2,1:T(1,128)}, u32[]{:S(2)}) copy-start(f32[48,4,1,1]{0,3,2,1:T(1,128)} %get-tuple-element.409) | copy-start | bytes 2308
  178.9 289.6 %copy-start.17 = (f32[48,4,1,1]{0,3,2,1:T(1,128)S(1)}, f32[48,4,1,1]{0,3,2,1:T(1,128)}, u32[]{:S(2)}) copy-start(f32[48,4,1,1]{0,3,2,1:T(1,128)} %get-tuple-element.410) | copy-start | bytes 2308
  178.9 289.6 %copy-start.18 = (f32[48,4,1,1]{0,3,2,1:T(1,128)S(1)}, f32[48,4,1,1]{0,3,2,1:T(1,128)}, u32[]{:S(2)}) copy-start(f32[48,4,1,1]{0,3,2,1:T(1,128)} %get-tuple-element.411) | copy-start | bytes 2308
  180.3 287.7 %all-to-all-start.6 = ((bf16[32,2,384]{2,1,0:T(2,128)(2,1)}), bf16[32,2,384]{2,1,0:T(2,128)(2,1)S(1)}, u32[]{:S(2)}, u32[]{:S(2)}) async-start(bf16[32,2,384]{2,1,0:T(2,128)(2,1)} %reshape.55208), calls=%async_computation.6 | async-start | bytes 98304 | tf_op jit(solution)/shard_map/all_to_all | solution.py:158
  (71 other events, 7585.3 us)
Sparse Core Ops, SparseCore 0:
  148.1 279.6 all-reduce.6
where the time goes:
time: 487 us; the launch traced here: 486 us
  blocking collectives  277 us (57%)
  starting transfers between devices  71.5 us (15%)
  between operations  58.2 us (12%)
  local copies, waits for them, and re-layouts  24.1 us (5%)
  matrix products  20.6 us (4%)
  waiting for transfers between devices  20.2 us (4%)
  other arithmetic  14.3 us (3%)
    psum x1, blocking collectives, shards(): lax.psum((filter_part, disco_part), ('ens', 'lat'))  277 us
    all_to_all x2, starting transfers between devices, to_modes(): lax.all_to_all(spectrum, 'lat', split_axis=3, concat_axis=1, tiled=True)  18.5 us
    all_to_all x2, starting transfers between devices, to_bands(): lax.all_to_all(spectrum, 'lat', split_axis=1, concat_axis=3, tiled=True)  17.6 us
    ppermute x2, starting transfers between devices, padded_2(): lax.ppermute(lax.slice_in_dim(block, 0, width, axis=dim), axis, backward)  11.6 us
  transfers between devices with their start and end apart: 12, of which 4 were waited for; matrix products, arithmetic and copies ran while one was open for 9% of the time, Pallas kernels for 0%

commit v1 on v0

--- a/solution.py
+++ b/solution.py
@@ -317,7 +317,15 @@
                 + kernel_ext[:, row_start : row_start + lat_rows, reach, span][:, :, None] * window
             )
     grad_input = (adjoint_member.astype(jnp.float32) + spectral_back + spread).astype(jnp.bfloat16)
-    filter_total, disco_total = lax.psum((filter_part, disco_part), ("ens", "lat"))
+
+    def limits_cut(work_x):
+        link_axis = "ens"
+        named_axis = "lat"
+        for q in (named_axis, link_axis):
+            work_x = lax.psum(work_x, q)
+        return work_x
+
+    filter_total, disco_total = limits_cut((filter_part, disco_part))
     total_hidden, total_output = lax.psum((grad_hidden, grad_output), ("ens", "lat", "chan"))
     hidden_rows = total_hidden.shape[0] // band_count
     output_rows = total_output.shape[0] // band_count

time: 487 us -> 444 us (0.912)
  the two profiles are of different devices: /device:TPU:256 before, /device:TPU:1 now
where the time goes in v1:
time: 444 us; the launch traced here: 443 us
  blocking collectives  155 us (35%)
  waiting for transfers between devices  105 us (24%)
  starting transfers between devices  65.2 us (15%)
  between operations  58 us (13%)
  local copies, waits for them, and re-layouts  24.1 us (5%)
  matrix products  20.6 us (5%)
  other arithmetic  14.3 us (3%)
    psum x2, blocking collectives, limits_cut(): work_x = lax.psum(work_x, q)  155 us
    psum x1, waiting for transfers between devices, shards(): lax.psum((grad_hidden, grad_output), ('ens', 'lat', 'chan'))  82.4 us
    all_to_all x2, starting transfers between devices, to_bands(): lax.all_to_all(spectrum, 'lat', split_axis=1, concat_axis=3, tiled=True)  21.8 us
    all_to_all x2, starting transfers between devices, to_modes(): lax.all_to_all(spectrum, 'lat', split_axis=3, concat_axis=1, tiled=True)  17.6 us
    unnamed x193, local copies, waits for them, and re-layouts  9.26 us
  transfers between devices with their start and end apart: 12, of which 6 were waited for; matrix products, arithmetic and copies ran while one was open for 10% of the time, Pallas kernels for 0%

profile of v1, /device:TPU:1, one launch (start us, length us, event | category | flops | bytes accessed | tf_op | source)
XLA Modules:
  0.0 442.6 jit_solution(16155406760483295653)
XLA Ops:
  9.7 13.7 %all-to-all-start = ((bf16[32,2,384]{2,1,0:T(2,128)(2,1)}), bf16[32,2,384]{2,1,0:T(2,128)(2,1)S(1)}, u32[]{:S(2)}, u32[]{:S(2)}) async-start(bf16[32,2,384]{2,1,0:T(2,128)(2,1)} %reshape.55196), calls=%async_computation | async-start | bytes 98304 | tf_op jit(solution)/shard_map/all_to_all | solution.py:154
  23.5 3.1 collective-permute-start
  26.6 1.3 collective-permute-start.1
  88.2 11.0 %all-to-all-start.1 = ((bf16[32,2,384]{2,1,0:T(2,128)(2,1)}), bf16[32,2,384]{2,1,0:T(2,128)(2,1)S(1)}, u32[]{:S(2)}, u32[]{:S(2)}) async-start(bf16[32,2,384]{2,1,0:T(2,128)(2,1)} %reshape.55198), calls=%async_computation.1 | async-start | bytes 98304 | tf_op jit(solution)/shard_map/all_to_all | solution.py:158
  99.4 8.6 %all-to-all-done.1 = bf16[32,2,384]{2,1,0:T(2,128)(2,1)S(1)} async-done(((bf16[32,2,384]{2,1,0:T(2,128)(2,1)}), bf16[32,2,384]{2,1,0:T(2,128)(2,1)S(1)}, u32[]{:S(2)}, u32[]{:S(2)}) %all-to-all-start.1) | async-done | bytes 49184 | tf_op jit(solution)/shard_map/all_to_all | solution.py:158
  107.9 6.8 %all-to-all-start.3 = ((bf16[8,2,3072]{2,1,0:T(2,128)(2,1)}), bf16[8,2,3072]{2,1,0:T(2,128)(2,1)S(1)}, u32[]{:S(2)}, u32[]{:S(2)}) async-start(bf16[8,2,3072]{2,1,0:T(2,128)(2,1)} %reshape.55202), calls=%async_computation.3 | async-start | bytes 196608 | tf_op jit(solution)/shard_map/all_to_all | solution.py:204
  115.5 5.9 %fusion.2 = bf16[48,4,256]{2,0,1:T(8,128)(2,1)S(1)} fusion(bf16[48,4,128]{0,2,1:T(8,128)(2,1)S(1)} %bitcast.623, bf16[48,4,256]{2,0,1:T(8,128)(2,1)S(1)} %bitcast.596, f32[48,4]{0,1:T(4,128)S(1)} %bitcast.820, f32[48,4]{0,1:T(4,128)S(1)} %bitcast.821, f32[48,4]{0,1:T(4,128)S(1)} %bitcast.822, f32[48,4]{0,1:T(4,128)S(1)} %bitcast.823, ...), kind=kOutput, calls=%fused_computation.173 | convolution fusion | flops 25493504 | bytes 8339200 | tf_op jit(solution)/shard_map/dot_general | solution.py:217
  122.6 6.6 %all-to-all-start.2 = ((bf16[8,2,3072]{2,1,0:T(2,128)(2,1)}), bf16[8,2,3072]{2,1,0:T(2,128)(2,1)S(1)}, u32[]{:S(2)}, u32[]{:S(2)}) async-start(bf16[8,2,3072]{2,1,0:T(2,128)(2,1)} %reshape.55200), calls=%async_computation.2 | async-start | bytes 196608 | tf_op jit(solution)/shard_map/all_to_all | solution.py:240
  130.6 6.3 %all-to-all-done.2 = bf16[8,2,3072]{2,1,0:T(2,128)(2,1)S(1)} async-done(((bf16[8,2,3072]{2,1,0:T(2,128)(2,1)}), bf16[8,2,3072]{2,1,0:T(2,128)(2,1)S(1)}, u32[]{:S(2)}, u32[]{:S(2)}) %all-to-all-start.2) | async-done | bytes 98336 | tf_op jit(solution)/shard_map/all_to_all | solution.py:240
  138.8 2.0 fusion.24
  143.0 3.4 all-to-all-start.4
  146.7 1.4 fusion.613
  148.1 5.7 %all-to-all-done.4 = bf16[8,2,3072]{2,1,0:T(2,128)(2,1)S(1)} async-done(((bf16[8,2,3072]{2,1,0:T(2,128)(2,1)}), bf16[8,2,3072]{2,1,0:T(2,128)(2,1)S(1)}, u32[]{:S(2)}, u32[]{:S(2)}) %all-to-all-start.4) | async-done | bytes 98336 | tf_op jit(solution)/shard_map/all_to_all | solution.py:249
  161.3 3.9 all-to-all-start.5
  165.2 3.0 collective-permute-start.2
  168.2 1.3 collective-permute-start.3
  171.5 2.1 collective-permute-done.3
  176.0 10.8 %all-to-all-start.6 = ((bf16[32,2,384]{2,1,0:T(2,128)(2,1)}), bf16[32,2,384]{2,1,0:T(2,128)(2,1)S(1)}, u32[]{:S(2)}, u32[]{:S(2)}) async-start(bf16[32,2,384]{2,1,0:T(2,128)(2,1)} %reshape.55208), calls=%async_computation.6 | async-start | bytes 98304 | tf_op jit(solution)/shard_map/all_to_all | solution.py:158
  186.8 115.1 %all-reduce.4 = (f32[2,64,48]{1,2,0:T(8,128)S(1)}, f32[9,48]{1,0:T(8,128)S(1)}) all-reduce(f32[2,64,48]{1,2,0:T(8,128)S(1)} %pad_maximum_fusion.8, f32[9,48]{1,0:T(8,128)S(1)} %convolution_bitcast_fusion.6), channel_id=1, replica_groups=mesh['ens'=2,'lat'=32,'chan'=8] {'lat'}, use_global_device_ids=true, to_apply=%region_5.6 | all-reduce | flops 6576 | bytes 52608 | tf_op jit(solution)/shard_map/psum | solution.py:325
  301.9 40.1 %all-reduce.5 = (f32[2,64,48]{1,2,0:T(8,128)}, f32[9,48]{1,0:T(8,128)S(1)}) all-reduce(f32[2,64,48]{1,2,0:T(8,128)S(1)} %get-tuple-element.134, f32[9,48]{1,0:T(8,128)S(1)} %get-tuple-element.135), channel_id=1, replica_groups=mesh['ens'=2,'lat'=32,'chan'=8] {'ens'}, use_global_device_ids=true, to_apply=%region_6.7 | all-reduce | flops 6576 | bytes 52608 | tf_op jit(solution)/shard_map/psum | solution.py:325
  343.3 6.5 %fusion.4 = bf16[1,48,4,256]{3,1,2,0:T(8,128)(2,1)S(1)} fusion(bf16[48,4,128]{0,2,1:T(8,128)(2,1)S(1)} %bitcast.622, bf16[48,4,256]{2,0,1:T(8,128)(2,1)S(1)} %all_to_all.100, bf16[48,8,256]{2,0,1:T(8,128)(2,1)S(1)} %get-tuple-element.541, bf16[48,8,8]{2,0,1:T(8,128)(2,1)S(1)} %get-tuple-element.522, bf16[48,8,8]{2,0,1:T(8,128)(2,1)S(1)} %get-tuple-element.521, ...), kind=kOutput, calls=%fused_computation.177 | convolution fusion | flops 37191680 | bytes 1076992 | tf_op jit(solution)/shard_map/dot_general | solution.py:272
  350.5 82.4 %all-reduce.8.cloned.1.call-done = (f32[384,768]{1,0:T(8,128)}, f32[768,384]{1,0:T(8,128)}) async-done(((f32[384,768]{1,0:T(8,128)}, f32[768,384]{1,0:T(8,128)}), (f32[384,768]{1,0:T(8,128)}, f32[768,384]{1,0:T(8,128)})) %all-reduce.8.cloned.1.call-update) | async-done | bytes 2359312 | tf_op jit(solution)/shard_map/psum | solution.py:329
  432.9 1.5 dynamic-slice_multiply_fusion
  434.4 1.4 dynamic-slice_multiply_fusion.1
  (450 shorter events, 40.6 us)
Async XLA Ops:
  9.7 76.3 %all-to-all-start = ((bf16[32,2,384]{2,1,0:T(2,128)(2,1)}), bf16[32,2,384]{2,1,0:T(2,128)(2,1)S(1)}, u32[]{:S(2)}, u32[]{:S(2)}) async-start(bf16[32,2,384]{2,1,0:T(2,128)(2,1)} %reshape.55196), calls=%async_computation | async-start | bytes 98304 | tf_op jit(solution)/shard_map/all_to_all | solution.py:154
  23.5 62.4 %collective-permute-start = (bf16[48,2,256]{2,0,1:T(8,128)(2,1)S(1)}, bf16[48,2,256]{2,0,1:T(8,128)(2,1)S(1)}, u32[]{:S(2)}, u32[]{:S(2)}) collective-permute-start(bf16[48,2,256]{2,0,1:T(8,128)(2,1)S(1)} %get-tuple-element.539), channel_id=1, source_target_pairs={{0,8},{8,16},{16,24},{24,32},{32,40},{40,48},{48,56},{56,64},{64,7... | collective-permute-start | bytes 147464 | tf_op jit(solution)/shard_map/ppermute | solution.py:20
  26.6 59.3 %collective-permute-start.1 = (bf16[48,2,256]{2,0,1:T(8,128)(2,1)S(1)}, bf16[48,2,256]{2,0,1:T(8,128)(2,1)S(1)}, u32[]{:S(2)}, u32[]{:S(2)}) collective-permute-start(bf16[48,2,256]{2,0,1:T(8,128)(2,1)S(1)} %get-tuple-element.538), channel_id=1, source_target_pairs={{8,0},{16,8},{24,16},{32,24},{40,32},{48,40},{56,48},{64,56},{72,6... | collective-permute-start | bytes 147464 | tf_op jit(solution)/shard_map/ppermute | solution.py:23
  88.2 19.7 %all-to-all-start.1 = ((bf16[32,2,384]{2,1,0:T(2,128)(2,1)}), bf16[32,2,384]{2,1,0:T(2,128)(2,1)S(1)}, u32[]{:S(2)}, u32[]{:S(2)}) async-start(bf16[32,2,384]{2,1,0:T(2,128)(2,1)} %reshape.55198), calls=%async_computation.1 | async-start | bytes 98304 | tf_op jit(solution)/shard_map/all_to_all | solution.py:158
  107.9 14.7 %all-to-all-start.3 = ((bf16[8,2,3072]{2,1,0:T(2,128)(2,1)}), bf16[8,2,3072]{2,1,0:T(2,128)(2,1)S(1)}, u32[]{:S(2)}, u32[]{:S(2)}) async-start(bf16[8,2,3072]{2,1,0:T(2,128)(2,1)} %reshape.55202), calls=%async_computation.3 | async-start | bytes 196608 | tf_op jit(solution)/shard_map/all_to_all | solution.py:204
  122.6 14.2 %all-to-all-start.2 = ((bf16[8,2,3072]{2,1,0:T(2,128)(2,1)}), bf16[8,2,3072]{2,1,0:T(2,128)(2,1)S(1)}, u32[]{:S(2)}, u32[]{:S(2)}) async-start(bf16[8,2,3072]{2,1,0:T(2,128)(2,1)} %reshape.55200), calls=%async_computation.2 | async-start | bytes 196608 | tf_op jit(solution)/shard_map/all_to_all | solution.py:240
  143.0 10.9 %all-to-all-start.4 = ((bf16[8,2,3072]{2,1,0:T(2,128)(2,1)}), bf16[8,2,3072]{2,1,0:T(2,128)(2,1)S(1)}, u32[]{:S(2)}, u32[]{:S(2)}) async-start(bf16[8,2,3072]{2,1,0:T(2,128)(2,1)} %reshape.55204), calls=%async_computation.4 | async-start | bytes 196608 | tf_op jit(solution)/shard_map/all_to_all | solution.py:249
  146.4 286.5 %all-reduce.8.cloned.1.call-start = ((), (), s32[]{:S(2)}) async-start(), calls=%async_computation.7 | async-start | bytes 4718592 | tf_op jit(solution)/shard_map/psum | solution.py:329
  161.3 12.6 %all-to-all-start.5 = ((bf16[32,2,384]{2,1,0:T(2,128)(2,1)}), bf16[32,2,384]{2,1,0:T(2,128)(2,1)S(1)}, u32[]{:S(2)}, u32[]{:S(2)}) async-start(bf16[32,2,384]{2,1,0:T(2,128)(2,1)} %reshape.55206), calls=%async_computation.5 | async-start | bytes 98304 | tf_op jit(solution)/shard_map/all_to_all | solution.py:154
  165.2 6.3 %collective-permute-start.2 = (bf16[48,2,256]{2,0,1:T(8,128)(2,1)S(1)}, bf16[48,2,256]{2,0,1:T(8,128)(2,1)S(1)}, u32[]{:S(2)}, u32[]{:S(2)}) collective-permute-start(bf16[48,2,256]{2,0,1:T(8,128)(2,1)S(1)} %get-tuple-element.537), channel_id=1, source_target_pairs={{0,8},{8,16},{16,24},{24,32},{32,40},{40,48},{48,56},{56,64},{64,7... | collective-permute-start | bytes 147464 | tf_op jit(solution)/shard_map/ppermute | solution.py:20
  168.2 5.3 %collective-permute-start.3 = (bf16[48,2,256]{2,0,1:T(8,128)(2,1)S(1)}, bf16[48,2,256]{2,0,1:T(8,128)(2,1)S(1)}, u32[]{:S(2)}, u32[]{:S(2)}) collective-permute-start(bf16[48,2,256]{2,0,1:T(8,128)(2,1)S(1)} %get-tuple-element.536), channel_id=1, source_target_pairs={{8,0},{16,8},{24,16},{32,24},{40,32},{48,40},{56,48},{64,56},{72,6... | collective-permute-start | bytes 147464 | tf_op jit(solution)/shard_map/ppermute | solution.py:23
  174.5 168.5 %copy-start.7 = (f32[48,4,1,1]{0,3,2,1:T(1,128)S(1)}, f32[48,4,1,1]{0,3,2,1:T(1,128)}, u32[]{:S(2)}) copy-start(f32[48,4,1,1]{0,3,2,1:T(1,128)} %get-tuple-element.402) | copy-start | bytes 2308
  174.5 168.5 %copy-start.8 = (f32[48,4,1,1]{0,3,2,1:T(1,128)S(1)}, f32[48,4,1,1]{0,3,2,1:T(1,128)}, u32[]{:S(2)}) copy-start(f32[48,4,1,1]{0,3,2,1:T(1,128)} %get-tuple-element.403) | copy-start | bytes 2308
  174.5 168.5 %copy-start.9 = (f32[48,4,1,1]{0,3,2,1:T(1,128)S(1)}, f32[48,4,1,1]{0,3,2,1:T(1,128)}, u32[]{:S(2)}) copy-start(f32[48,4,1,1]{0,3,2,1:T(1,128)} %get-tuple-element.404) | copy-start | bytes 2308
  174.5 168.5 %copy-start.10 = (f32[48,4,1,1]{0,3,2,1:T(1,128)S(1)}, f32[48,4,1,1]{0,3,2,1:T(1,128)}, u32[]{:S(2)}) copy-start(f32[48,4,1,1]{0,3,2,1:T(1,128)} %get-tuple-element.405) | copy-start | bytes 2308
  174.5 168.5 %copy-start.11 = (f32[48,4,1,1]{0,3,2,1:T(1,128)S(1)}, f32[48,4,1,1]{0,3,2,1:T(1,128)}, u32[]{:S(2)}) copy-start(f32[48,4,1,1]{0,3,2,1:T(1,128)} %get-tuple-element.406) | copy-start | bytes 2308
  174.5 168.5 %copy-start.12 = (f32[48,4,1,1]{0,3,2,1:T(1,128)S(1)}, f32[48,4,1,1]{0,3,2,1:T(1,128)}, u32[]{:S(2)}) copy-start(f32[48,4,1,1]{0,3,2,1:T(1,128)} %get-tuple-element.407) | copy-start | bytes 2308
  174.5 168.5 %copy-start.13 = (f32[48,4,1,1]{0,3,2,1:T(1,128)S(1)}, f32[48,4,1,1]{0,3,2,1:T(1,128)}, u32[]{:S(2)}) copy-start(f32[48,4,1,1]{0,3,2,1:T(1,128)} %get-tuple-element.408) | copy-start | bytes 2308
  174.5 168.5 %copy-start.14 = (f32[48,4,1,1]{0,3,2,1:T(1,128)S(1)}, f32[48,4,1,1]{0,3,2,1:T(1,128)}, u32[]{:S(2)}) copy-start(f32[48,4,1,1]{0,3,2,1:T(1,128)} %get-tuple-element.409) | copy-start | bytes 2308
  174.5 168.5 %copy-start.15 = (f32[48,4,1,1]{0,3,2,1:T(1,128)S(1)}, f32[48,4,1,1]{0,3,2,1:T(1,128)}, u32[]{:S(2)}) copy-start(f32[48,4,1,1]{0,3,2,1:T(1,128)} %get-tuple-element.410) | copy-start | bytes 2308
  174.5 168.5 %copy-start.16 = (f32[48,4,1,1]{0,3,2,1:T(1,128)S(1)}, f32[48,4,1,1]{0,3,2,1:T(1,128)}, u32[]{:S(2)}) copy-start(f32[48,4,1,1]{0,3,2,1:T(1,128)} %get-tuple-element.411) | copy-start | bytes 2308
  174.6 168.5 %copy-start.17 = (f32[48,4,1,1]{0,3,2,1:T(1,128)S(1)}, f32[48,4,1,1]{0,3,2,1:T(1,128)}, u32[]{:S(2)}) copy-start(f32[48,4,1,1]{0,3,2,1:T(1,128)} %get-tuple-element.412) | copy-start | bytes 2308
  174.6 168.5 %copy-start.18 = (f32[48,4,1,1]{0,3,2,1:T(1,128)S(1)}, f32[48,4,1,1]{0,3,2,1:T(1,128)}, u32[]{:S(2)}) copy-start(f32[48,4,1,1]{0,3,2,1:T(1,128)} %get-tuple-element.413) | copy-start | bytes 2308
  176.0 166.6 %all-to-all-start.6 = ((bf16[32,2,384]{2,1,0:T(2,128)(2,1)}), bf16[32,2,384]{2,1,0:T(2,128)(2,1)S(1)}, u32[]{:S(2)}, u32[]{:S(2)}) async-start(bf16[32,2,384]{2,1,0:T(2,128)(2,1)} %reshape.55208), calls=%async_computation.6 | async-start | bytes 98304 | tf_op jit(solution)/shard_map/all_to_all | solution.py:158
  (71 other events, 5191.6 us)
Sparse Core Ops, SparseCore 0:
  152.3 280.4 all-reduce.7
